TPU v7x, 512 devices: a whole 4x4x16 slice. The times are simulated.
512 devices in a mesh: frame: 16 (over x, z_hi, core), space: 32 (over z_lo, y).
Axes of the slice: x: 4, y: 4, z: 16 (z_hi: 2, z_lo: 8; z = z_hi * 8 + z_lo), core: 2. Of those that a mesh axis runs over, the one named last changes fastest.
Arguments:
- q_space: bfloat16 [32, 2048, 1536], P('frame', 'space'), may hold values from -28 to 28
- k_space: bfloat16 [32, 2048, 1536], P('frame', 'space'), may hold values from -28 to 28
- v_space: bfloat16 [32, 2048, 1536], P('frame', 'space'), may hold values from -6 to 6
- q_time: bfloat16 [32, 2048, 1536], P('frame', 'space'), may hold values from -28 to 28
- k_time: bfloat16 [32, 2048, 1536], P('frame', 'space'), may hold values from -28 to 28
- v_time: bfloat16 [32, 2048, 1536], P('frame', 'space'), may hold values from -6 to 6
- out_grad: bfloat16 [32, 2048, 1536], P('frame', 'space'), may hold values from -6 to 6
- key_gain_space: float32 [1536], replicated, may hold values from 0.25 to 1.75
- value_gain_space: float32 [1536], replicated, may hold values from 0.25 to 1.75
- key_gain_time: float32 [1536], replicated, may hold values from 0.25 to 1.75
- value_gain_time: float32 [1536], replicated, may hold values from 0.25 to 1.75
Outputs:
- q_grad_space: bfloat16 [32, 2048, 1536], P('frame', 'space')
- k_grad_space: bfloat16 [32, 2048, 1536], P('frame', 'space')
- v_grad_space: bfloat16 [32, 2048, 1536], P('frame', 'space')
- q_grad_time: bfloat16 [32, 2048, 1536], P('frame', 'space')
- k_grad_time: bfloat16 [32, 2048, 1536], P('frame', 'space')
- v_grad_time: bfloat16 [32, 2048, 1536], P('frame', 'space')
- ia3_grads: float32 [4, 1536], replicated
All inputs are finite; a program needn't handle non-finite values.
Results may differ from a plain program's by a relative error of at most 0.003.
The roundings to bfloat16 on the way count: a program that leaves them out, or rounds other values in their place, can miss the bound.
Values may be sent and summed in bfloat16 or wider, within the bound.
A program may use at most 64 MiB of HBM per device.

v0:
```python
import jax
import jax.numpy as jnp
from jax import lax
from jax.sharding import PartitionSpec as P

H = 16


def attend_back(query_matrix, key_matrix, value_matrix, gradient_lines):
    items, length, head_size = query_matrix.shape
    logit_scale = head_size ** (-0.5)
    block = 512 if length % 512 == 0 and length > 512 else length
    blocks = length // block
    query_blocks = query_matrix.reshape(items, blocks, block, head_size).transpose(1, 0, 2, 3)
    grad_blocks = gradient_lines.reshape(items, blocks, block, head_size).transpose(1, 0, 2, 3)

    def one_block(carry, pair):
        key_acc, value_acc = carry
        query_part, grad_part = pair
        score_matrix = (
            jnp.einsum("ild,imd->ilm", query_part, key_matrix, preferred_element_type=jnp.float32)
            * logit_scale
        )
        row_max = jnp.max(score_matrix, axis=-1, keepdims=True)
        exp_terms = jnp.exp(score_matrix - row_max)
        probs_f = exp_terms / jnp.sum(exp_terms, axis=-1, keepdims=True)
        probabilities_narrow = probs_f.astype(jnp.bfloat16)
        value_acc = value_acc + jnp.einsum(
            "ilm,ild->imd", probabilities_narrow, grad_part, preferred_element_type=jnp.float32
        )
        probability_gradient = jnp.einsum(
            "ild,imd->ilm", grad_part, value_matrix, preferred_element_type=jnp.float32
        )
        row_delta = jnp.sum(probs_f * probability_gradient, axis=-1, keepdims=True)
        score_gradient = (probs_f * (probability_gradient - row_delta) * logit_scale).astype(
            jnp.bfloat16
        )
        query_part_grad = jnp.einsum(
            "ilm,imd->ild", score_gradient, key_matrix, preferred_element_type=jnp.float32
        ).astype(jnp.bfloat16)
        key_acc = key_acc + jnp.einsum(
            "ilm,ild->imd", score_gradient, query_part, preferred_element_type=jnp.float32
        )
        return ((key_acc, value_acc), query_part_grad)

    empty = jnp.zeros((items, length, head_size), jnp.float32)
    (key_acc, value_acc), query_parts = lax.scan(
        one_block, (empty, empty), (query_blocks, grad_blocks)
    )
    query_gradient = query_parts.transpose(1, 0, 2, 3).reshape(items, length, head_size)
    return (query_gradient, key_acc.astype(jnp.bfloat16), value_acc.astype(jnp.bfloat16))


def space_block(members):
    results = attend_back(members[0][0], members[1][0], members[2][0], members[3][0])
    return tuple((result[None] for result in results))


def time_block(members):
    turned = [member[:, 0].transpose(1, 0, 2) for member in members]
    results = attend_back(turned[0], turned[1], turned[2], turned[3])
    return tuple((result.transpose(1, 0, 2)[:, None] for result in results))


def space_items(tensor, parts, head_count):
    frames_local, space_local, model_width = tensor.shape
    head_size = model_width // head_count
    split = tensor.reshape(frames_local, space_local, head_count, head_size).transpose(0, 2, 1, 3)
    return split.reshape(parts, frames_local * head_count // parts, space_local, head_size)


def space_tokens(tensor, frames_local, head_count):
    head_size = tensor.shape[-1]
    space_local = tensor.shape[2]
    joined = tensor.reshape(frames_local, head_count, space_local, head_size).transpose(0, 2, 1, 3)
    return joined.reshape(frames_local, space_local, head_count * head_size)


def time_items(tensor, parts, head_count):
    frames_local, space_local, model_width = tensor.shape
    head_size = model_width // head_count
    return tensor.reshape(frames_local, parts, space_local * head_count // parts, head_size)


def scaled(tensor, gain):
    return (tensor.astype(jnp.float32) * gain).astype(jnp.bfloat16)


def gain_terms(gradient_lines, inputs):
    return jnp.sum(gradient_lines.astype(jnp.float32) * inputs.astype(jnp.float32), axis=(0, 1))


def shards(
    q_space,
    k_space,
    v_space,
    q_time,
    k_time,
    v_time,
    out_grad,
    key_gain_space,
    value_gain_space,
    key_gain_time,
    value_gain_time,
):
    frames_local, space_local, model_width = q_space.shape
    n_space = lax.axis_size("space")
    n_frame = lax.axis_size("frame")
    key_scaled = scaled(k_space, key_gain_space)
    value_scaled = scaled(v_space, value_gain_space)
    query_items = space_items(q_space, n_space, H)
    key_items = space_items(key_scaled, n_space, H)
    value_items = space_items(value_scaled, n_space, H)
    grad_items = space_items(out_grad, n_space, H)
    query_gradient, key_gradient, value_gradient = space_block(
        (
            lax.all_to_all(query_items, "space", split_axis=0, concat_axis=2, tiled=True),
            lax.all_to_all(key_items, "space", split_axis=0, concat_axis=2, tiled=True),
            lax.all_to_all(value_items, "space", split_axis=0, concat_axis=2, tiled=True),
            lax.all_to_all(grad_items, "space", split_axis=0, concat_axis=2, tiled=True),
        )
    )
    query_back = lax.all_to_all(query_gradient, "space", split_axis=2, concat_axis=0, tiled=True)
    key_back = lax.all_to_all(key_gradient, "space", split_axis=2, concat_axis=0, tiled=True)
    value_back = lax.all_to_all(value_gradient, "space", split_axis=2, concat_axis=0, tiled=True)
    query_back = space_tokens(query_back, frames_local, H)
    key_back = space_tokens(key_back, frames_local, H)
    value_back = space_tokens(value_back, frames_local, H)
    key_term = gain_terms(key_back, k_space)
    value_term = gain_terms(value_back, v_space)
    key_term, value_term = lax.psum((key_term, value_term), ("frame", "space"))
    key_scaled = scaled(k_time, key_gain_time)
    value_scaled = scaled(v_time, value_gain_time)
    query_items = time_items(q_time, n_frame, H)
    key_items = time_items(key_scaled, n_frame, H)
    value_items = time_items(value_scaled, n_frame, H)
    grad_items = time_items(out_grad, n_frame, H)
    query_gradient, key_gradient, value_gradient = time_block(
        (
            lax.all_to_all(query_items, "frame", split_axis=1, concat_axis=0, tiled=True),
            lax.all_to_all(key_items, "frame", split_axis=1, concat_axis=0, tiled=True),
            lax.all_to_all(value_items, "frame", split_axis=1, concat_axis=0, tiled=True),
            lax.all_to_all(grad_items, "frame", split_axis=1, concat_axis=0, tiled=True),
        )
    )
    time_query_back = lax.all_to_all(
        query_gradient, "frame", split_axis=0, concat_axis=1, tiled=True
    )
    time_key_back = lax.all_to_all(key_gradient, "frame", split_axis=0, concat_axis=1, tiled=True)
    time_value_back = lax.all_to_all(
        value_gradient, "frame", split_axis=0, concat_axis=1, tiled=True
    )
    time_query_back = time_query_back.reshape(frames_local, space_local, model_width)
    time_key_back = time_key_back.reshape(frames_local, space_local, model_width)
    time_value_back = time_value_back.reshape(frames_local, space_local, model_width)
    time_key_term = gain_terms(time_key_back, k_time)
    time_value_term = gain_terms(time_value_back, v_time)
    time_key_term, time_value_term = lax.psum((time_key_term, time_value_term), ("frame", "space"))
    space_kt, space_vt, time_kt, time_vt = (key_term, value_term, time_key_term, time_value_term)
    total_tokens = frames_local * n_frame * space_local * n_space
    norm_factor = float(total_tokens) ** (-0.5)
    ia3_grads = jnp.stack([space_kt, space_vt, time_kt, time_vt]) * norm_factor
    return (
        query_back,
        scaled(key_back, key_gain_space),
        scaled(value_back, value_gain_space),
        time_query_back,
        scaled(time_key_back, key_gain_time),
        scaled(time_value_back, value_gain_time),
        ia3_grads,
    )


def solution(mesh):
    return jax.shard_map(
        shards,
        mesh=mesh,
        in_specs=(
            P("frame", "space", None),
            P("frame", "space", None),
            P("frame", "space", None),
            P("frame", "space", None),
            P("frame", "space", None),
            P("frame", "space", None),
            P("frame", "space", None),
            P(),
            P(),
            P(),
            P(),
        ),
        out_specs=(
            P("frame", "space", None),
            P("frame", "space", None),
            P("frame", "space", None),
            P("frame", "space", None),
            P("frame", "space", None),
            P("frame", "space", None),
            P(),
        ),
        check_vma=False,
    )
```

profile of v0, /device:TPU:1, one launch (start us, length us, event | category | flops | bytes accessed | tf_op | source)
XLA Modules:
  0.0 648.7 jit_solution(14525521670941211730)
XLA Ops:
  3.6 19.1 %all-to-all-start.7 = ((bf16[2,16,64,96]{3,0,2,1:T(2,128)(2,1)}), bf16[2,16,64,96]{3,0,2,1:T(2,128)(2,1)S(1)}, u32[]{:S(2)}, u32[]{:S(2)}) async-start(bf16[2,16,64,96]{3,0,2,1:T(2,128)(2,1)} %copy.112), calls=%async_computation.7 | async-start | bytes 1048576 | tf_op jit(solution)/shard_map/all_to_all | solution.py:141
  25.4 16.5 %all-to-all-done.7 = bf16[2,16,64,96]{3,0,2,1:T(2,128)(2,1)S(1)} async-done(((bf16[2,16,64,96]{3,0,2,1:T(2,128)(2,1)}), bf16[2,16,64,96]{3,0,2,1:T(2,128)(2,1)S(1)}, u32[]{:S(2)}, u32[]{:S(2)}) %all-to-all-start.7) | async-done | bytes 393248 | tf_op jit(solution)/shard_map/all_to_all | solution.py:141
  42.0 4.2 all-to-all-start.10
  48.0 16.8 %all-to-all-done.10 = bf16[2,16,64,96]{3,0,2,1:T(2,128)(2,1)S(1)} async-done(((bf16[2,16,64,96]{3,0,2,1:T(2,128)(2,1)}), bf16[2,16,64,96]{3,0,2,1:T(2,128)(2,1)S(1)}, u32[]{:S(2)}, u32[]{:S(2)}) %all-to-all-start.10) | async-done | bytes 393248 | tf_op jit(solution)/shard_map/all_to_all | solution.py:143
  64.8 8.1 %all-to-all-start.8 = ((bf16[2,16,64,96]{3,0,2,1:T(2,128)(2,1)}), bf16[2,16,64,96]{3,0,2,1:T(2,128)(2,1)S(1)}, u32[]{:S(2)}, u32[]{:S(2)}) async-start(bf16[2,16,64,96]{3,0,2,1:T(2,128)(2,1)} %copy.114), calls=%async_computation.8 | async-start | bytes 1048576 | tf_op jit(solution)/shard_map/all_to_all | solution.py:140
  74.3 18.3 %all-to-all-done.8 = bf16[2,16,64,96]{3,0,2,1:T(2,128)(2,1)S(1)} async-done(((bf16[2,16,64,96]{3,0,2,1:T(2,128)(2,1)}), bf16[2,16,64,96]{3,0,2,1:T(2,128)(2,1)S(1)}, u32[]{:S(2)}, u32[]{:S(2)}) %all-to-all-start.8) | async-done | bytes 393248 | tf_op jit(solution)/shard_map/all_to_all | solution.py:140
  92.5 28.2 %all-to-all-start = ((bf16[32,1,64,96]{3,2,1,0:T(8,128)(2,1)}), bf16[32,1,64,96]{3,2,1,0:T(8,128)(2,1)}, u32[]{:S(2)}, u32[]{:S(2)}) async-start(bf16[32,1,64,96]{3,2,1,0:T(8,128)(2,1)} %bitcast.1), calls=%async_computation | async-start | bytes 1048576 | tf_op jit(solution)/shard_map/all_to_all | solution.py:117
  122.2 25.3 %all-to-all-done = bf16[32,1,64,96]{3,2,1,0:T(8,128)(2,1)} async-done(((bf16[32,1,64,96]{3,2,1,0:T(8,128)(2,1)}), bf16[32,1,64,96]{3,2,1,0:T(8,128)(2,1)}, u32[]{:S(2)}, u32[]{:S(2)}) %all-to-all-start) | async-done | bytes 393248 | tf_op jit(solution)/shard_map/all_to_all | solution.py:117
  147.5 8.7 %all-to-all-start.1 = ((bf16[32,1,64,96]{3,2,1,0:T(8,128)(2,1)}), bf16[32,1,64,96]{3,2,1,0:T(8,128)(2,1)S(1)}, u32[]{:S(2)}, u32[]{:S(2)}) async-start(bf16[32,1,64,96]{3,2,1,0:T(8,128)(2,1)} %bitcast.6), calls=%async_computation.1 | async-start | bytes 1048576 | tf_op jit(solution)/shard_map/all_to_all | solution.py:118
  157.7 25.3 %all-to-all-done.1 = bf16[32,1,64,96]{3,2,1,0:T(8,128)(2,1)S(1)} async-done(((bf16[32,1,64,96]{3,2,1,0:T(8,128)(2,1)}), bf16[32,1,64,96]{3,2,1,0:T(8,128)(2,1)S(1)}, u32[]{:S(2)}, u32[]{:S(2)}) %all-to-all-start.1) | async-done | bytes 393248 | tf_op jit(solution)/shard_map/all_to_all | solution.py:118
  183.0 8.9 %all-to-all-start.2 = ((bf16[32,1,64,96]{3,2,1,0:T(8,128)(2,1)}), bf16[32,1,64,96]{3,2,1,0:T(8,128)(2,1)}, u32[]{:S(2)}, u32[]{:S(2)}) async-start(bf16[32,1,64,96]{3,2,1,0:T(8,128)(2,1)} %bitcast.9), calls=%async_computation.2 | async-start | bytes 1048576 | tf_op jit(solution)/shard_map/all_to_all | solution.py:120
  194.4 24.2 %all-to-all-done.2 = bf16[32,1,64,96]{3,2,1,0:T(8,128)(2,1)} async-done(((bf16[32,1,64,96]{3,2,1,0:T(8,128)(2,1)}), bf16[32,1,64,96]{3,2,1,0:T(8,128)(2,1)}, u32[]{:S(2)}, u32[]{:S(2)}) %all-to-all-start.2) | async-done | bytes 393248 | tf_op jit(solution)/shard_map/all_to_all | solution.py:120
  218.6 8.9 %all-to-all-start.3 = ((bf16[32,1,64,96]{3,2,1,0:T(8,128)(2,1)}), bf16[32,1,64,96]{3,2,1,0:T(8,128)(2,1)}, u32[]{:S(2)}, u32[]{:S(2)}) async-start(bf16[32,1,64,96]{3,2,1,0:T(8,128)(2,1)} %bitcast.14), calls=%async_computation.3 | async-start | bytes 1048576 | tf_op jit(solution)/shard_map/all_to_all | solution.py:119
  232.7 21.5 %all-to-all-done.3 = bf16[32,1,64,96]{3,2,1,0:T(8,128)(2,1)} async-done(((bf16[32,1,64,96]{3,2,1,0:T(8,128)(2,1)}), bf16[32,1,64,96]{3,2,1,0:T(8,128)(2,1)}, u32[]{:S(2)}, u32[]{:S(2)}) %all-to-all-start.3) | async-done | bytes 393248 | tf_op jit(solution)/shard_map/all_to_all | solution.py:119
  254.3 13.9 %all-to-all-start.13 = ((bf16[32,1,64,96]{3,2,1,0:T(8,128)(2,1)}), bf16[32,1,64,96]{3,2,1,0:T(8,128)(2,1)}, u32[]{:S(2)}, u32[]{:S(2)}) async-start(bf16[32,1,64,96]{3,2,1,0:T(8,128)(2,1)} %copy.126), calls=%async_computation.13 | async-start | bytes 1048576 | tf_op jit(solution)/shard_map/all_to_all | solution.py:150
  268.2 52.0 %while.3 = (s32[]{:T(128)}, f32[1,2048,96]{1,2,0:T(8,128)S(1)}, f32[1,2048,96]{1,2,0:T(8,128)}, bf16[4,1,512,96]{2,3,1,0:T(8,128)(2,1)}, bf16[4,1,512,96]{3,2,1,...) while((s32[]{:T(128)}, f32[1,2048,96]{1,2,0:T(8,128)S(1)}, ...), condition=%wide.region_4.5_spmd.clone, body=%wide.region_0.4_spmd.clone.sunk | while | flops 1029487104 | bytes 80599304 | solution.py:47
  322.2 11.7 %reduce.6 = bf16[2048,96]{1,0:T(8,128)(2,1)S(1)} reduce(bf16[2048,1,1,96]{3,2,1,0:T(2,128)(2,1)S(1)} %bitcast.194, bf16[]{:T(256)} %broadcast.60), dimensions={1,2}, to_apply=%bitcast.144.reduce_sub_computation | reduce | bytes 786434
  335.5 5.8 all-to-all-start.4
  343.3 11.5 %reduce.7 = bf16[2048,96]{1,0:T(8,128)(2,1)S(1)} reduce(bf16[2048,1,1,96]{3,2,1,0:T(2,128)(2,1)S(1)} %bitcast.196, bf16[]{:T(256)} %broadcast.60), dimensions={1,2}, to_apply=%bitcast.146.reduce_sub_computation | reduce | bytes 786434
  356.5 7.5 %all-to-all-done.4 = bf16[32,2,3072]{2,1,0:T(2,128)(2,1)S(1)} async-done(((bf16[32,2,3072]{2,1,0:T(2,128)(2,1)}), bf16[32,2,3072]{2,1,0:T(2,128)(2,1)S(1)}, u32[]{:S(2)}, u32[]{:S(2)}) %all-to-all-start.4) | async-done | bytes 393248 | tf_op jit(solution)/shard_map/all_to_all | solution.py:123
  364.0 7.3 %all-to-all-start.5 = ((bf16[32,2,3072]{2,1,0:T(2,128)(2,1)}), bf16[32,2,3072]{2,1,0:T(2,128)(2,1)S(1)}, u32[]{:S(2)}, u32[]{:S(2)}) async-start(bf16[32,2,3072]{2,1,0:T(2,128)(2,1)} %reshape.215), calls=%async_computation.5 | async-start | bytes 786432 | tf_op jit(solution)/shard_map/all_to_all | solution.py:124
  377.3 14.1 %all-to-all-done.5 = bf16[32,2,3072]{2,1,0:T(2,128)(2,1)S(1)} async-done(((bf16[32,2,3072]{2,1,0:T(2,128)(2,1)}), bf16[32,2,3072]{2,1,0:T(2,128)(2,1)S(1)}, u32[]{:S(2)}, u32[]{:S(2)}) %all-to-all-start.5) | async-done | bytes 393248 | tf_op jit(solution)/shard_map/all_to_all | solution.py:124
  391.4 19.5 %all-to-all-start.9 = ((bf16[2,16,64,96]{3,0,2,1:T(2,128)(2,1)}), bf16[2,16,64,96]{3,0,2,1:T(2,128)(2,1)S(1)}, u32[]{:S(2)}, u32[]{:S(2)}) async-start(bf16[2,16,64,96]{3,0,2,1:T(2,128)(2,1)} %copy.117), calls=%async_computation.9 | async-start | bytes 1048576 | tf_op jit(solution)/shard_map/all_to_all | solution.py:142
  411.7 11.5 %reduce.8 = bf16[2048,96]{1,0:T(8,128)(2,1)S(1)} reduce(bf16[2048,1,1,96]{3,2,1,0:T(2,128)(2,1)S(1)} %bitcast.195, bf16[]{:T(256)} %broadcast.60), dimensions={1,2}, to_apply=%bitcast.148.reduce_sub_computation | reduce | bytes 786434
  424.8 10.8 %all-to-all-done.9 = bf16[2,16,64,96]{3,0,2,1:T(2,128)(2,1)S(1)} async-done(((bf16[2,16,64,96]{3,0,2,1:T(2,128)(2,1)}), bf16[2,16,64,96]{3,0,2,1:T(2,128)(2,1)S(1)}, u32[]{:S(2)}, u32[]{:S(2)}) %all-to-all-start.9) | async-done | bytes 393248 | tf_op jit(solution)/shard_map/all_to_all | solution.py:142
  435.6 15.1 %all-to-all-start.6 = ((bf16[32,2,3072]{2,1,0:T(2,128)(2,1)}), bf16[32,2,3072]{2,1,0:T(2,128)(2,1)S(1)}, u32[]{:S(2)}, u32[]{:S(2)}) async-start(bf16[32,2,3072]{2,1,0:T(2,128)(2,1)} %reshape.217), calls=%async_computation.6 | async-start | bytes 786432 | tf_op jit(solution)/shard_map/all_to_all | solution.py:125
  454.9 16.0 %all-to-all-done.6 = bf16[32,2,3072]{2,1,0:T(2,128)(2,1)S(1)} async-done(((bf16[32,2,3072]{2,1,0:T(2,128)(2,1)}), bf16[32,2,3072]{2,1,0:T(2,128)(2,1)S(1)}, u32[]{:S(2)}, u32[]{:S(2)}) %all-to-all-start.6) | async-done | bytes 393248 | tf_op jit(solution)/shard_map/all_to_all | solution.py:125
  471.6 8.4 %all-to-all-start.11 = ((bf16[32,1,64,96]{3,2,1,0:T(8,128)(2,1)}), bf16[32,1,64,96]{3,2,1,0:T(8,128)(2,1)S(1)}, u32[]{:S(2)}, u32[]{:S(2)}) async-start(bf16[32,1,64,96]{3,2,1,0:T(8,128)(2,1)} %copy.122), calls=%async_computation.11 | async-start | bytes 1048576 | tf_op jit(solution)/shard_map/all_to_all | solution.py:146
  483.1 22.0 %all-to-all-done.11 = bf16[32,1,64,96]{3,2,1,0:T(8,128)(2,1)S(1)} async-done(((bf16[32,1,64,96]{3,2,1,0:T(8,128)(2,1)}), bf16[32,1,64,96]{3,2,1,0:T(8,128)(2,1)S(1)}, u32[]{:S(2)}, u32[]{:S(2)}) %all-to-all-start.11) | async-done | bytes 393248 | tf_op jit(solution)/shard_map/all_to_all | solution.py:146
  505.9 4.6 all-to-all-start.12
  523.0 6.4 all-to-all-done.12
  530.9 116.6 %all-reduce = (f32[1,1536]{1,0:T(1,128)S(1)}, f32[1,1536]{1,0:T(1,128)S(1)}, f32[1,1536]{1,0:T(1,128)S(1)}, f32[1,1536]{1,0:T(1,128)S(1)}) all-reduce(f32[1,1536]{1,0:T(1,128)S(1)} %copy-done.24, f32[1,1536]{1,0:T(1,128)S(1)} %stack.17, f32[1,1536]{1,0:T(1,128)S(1)} %stack.16, ...), channel_id=1, replica_groups=mesh['frame'=16,'space'=32] {'frame','space'}, use_global_device_ids=true, to_apply=%region_15.16 | all-reduce | flops 6144 | bytes 49152 | tf_op jit(solution)/shard_map/psum | solution.py:158
  (181 shorter events, 109.7 us)
Async XLA Ops:
  0.6 45.5 %copy-start.18 = (bf16[2,64,1536]{2,1,0:T(8,128)(2,1)S(1)}, bf16[2,64,1536]{2,1,0:T(8,128)(2,1)}, u32[]{:S(2)}) copy-start(bf16[2,64,1536]{2,1,0:T(8,128)(2,1)} %param.16) | copy-start | bytes 1179652
  2.2 70.6 %copy-start.19 = (bf16[2,64,1536]{2,1,0:T(8,128)(2,1)S(1)}, bf16[2,64,1536]{2,1,0:T(8,128)(2,1)}, u32[]{:S(2)}) copy-start(bf16[2,64,1536]{2,1,0:T(8,128)(2,1)} %param.13) | copy-start | bytes 1179652
  3.6 38.4 %all-to-all-start.7 = ((bf16[2,16,64,96]{3,0,2,1:T(2,128)(2,1)}), bf16[2,16,64,96]{3,0,2,1:T(2,128)(2,1)S(1)}, u32[]{:S(2)}, u32[]{:S(2)}) async-start(bf16[2,16,64,96]{3,0,2,1:T(2,128)(2,1)} %copy.112), calls=%async_computation.7 | async-start | bytes 1048576 | tf_op jit(solution)/shard_map/all_to_all | solution.py:141
  24.1 96.6 %copy-start.7 = (bf16[2,64,1536]{2,1,0:T(8,128)(2,1)S(1)}, bf16[2,64,1536]{2,1,0:T(8,128)(2,1)}, u32[]{:S(2)}) copy-start(bf16[2,64,1536]{2,1,0:T(8,128)(2,1)} %param.14) | copy-start | bytes 1179652
  24.1 96.6 %copy-start.21 = (f32[1536]{0:T(1024)S(1)}, f32[1536]{0:T(1024)}, u32[]{:S(2)}) copy-start(f32[1536]{0:T(1024)} %param.20) | copy-start | bytes 18436
  42.0 22.8 %all-to-all-start.10 = ((bf16[2,16,64,96]{3,0,2,1:T(2,128)(2,1)}), bf16[2,16,64,96]{3,0,2,1:T(2,128)(2,1)S(1)}, u32[]{:S(2)}, u32[]{:S(2)}) async-start(bf16[2,16,64,96]{3,0,2,1:T(2,128)(2,1)} %copy.119), calls=%async_computation.10 | async-start | bytes 1048576 | tf_op jit(solution)/shard_map/all_to_all | solution.py:143
  48.0 108.3 %copy-start.5 = (bf16[2,64,1536]{2,1,0:T(8,128)(2,1)S(1)}, bf16[2,64,1536]{2,1,0:T(8,128)(2,1)}, u32[]{:S(2)}) copy-start(bf16[2,64,1536]{2,1,0:T(8,128)(2,1)} %param.19) | copy-start | bytes 1179652
  64.8 27.8 %all-to-all-start.8 = ((bf16[2,16,64,96]{3,0,2,1:T(2,128)(2,1)}), bf16[2,16,64,96]{3,0,2,1:T(2,128)(2,1)S(1)}, u32[]{:S(2)}, u32[]{:S(2)}) async-start(bf16[2,16,64,96]{3,0,2,1:T(2,128)(2,1)} %copy.114), calls=%async_computation.8 | async-start | bytes 1048576 | tf_op jit(solution)/shard_map/all_to_all | solution.py:140
  74.3 117.7 %copy-start.20 = (f32[1536]{0:T(1024)S(1)}, f32[1536]{0:T(1024)}, u32[]{:S(2)}) copy-start(f32[1536]{0:T(1024)} %param.21) | copy-start | bytes 18436
  92.5 55.0 %all-to-all-start = ((bf16[32,1,64,96]{3,2,1,0:T(8,128)(2,1)}), bf16[32,1,64,96]{3,2,1,0:T(8,128)(2,1)}, u32[]{:S(2)}, u32[]{:S(2)}) async-start(bf16[32,1,64,96]{3,2,1,0:T(8,128)(2,1)} %bitcast.1), calls=%async_computation | async-start | bytes 1048576 | tf_op jit(solution)/shard_map/all_to_all | solution.py:117
  147.5 35.5 %all-to-all-start.1 = ((bf16[32,1,64,96]{3,2,1,0:T(8,128)(2,1)}), bf16[32,1,64,96]{3,2,1,0:T(8,128)(2,1)S(1)}, u32[]{:S(2)}, u32[]{:S(2)}) async-start(bf16[32,1,64,96]{3,2,1,0:T(8,128)(2,1)} %bitcast.6), calls=%async_computation.1 | async-start | bytes 1048576 | tf_op jit(solution)/shard_map/all_to_all | solution.py:118
  183.0 35.6 %all-to-all-start.2 = ((bf16[32,1,64,96]{3,2,1,0:T(8,128)(2,1)}), bf16[32,1,64,96]{3,2,1,0:T(8,128)(2,1)}, u32[]{:S(2)}, u32[]{:S(2)}) async-start(bf16[32,1,64,96]{3,2,1,0:T(8,128)(2,1)} %bitcast.9), calls=%async_computation.2 | async-start | bytes 1048576 | tf_op jit(solution)/shard_map/all_to_all | solution.py:120
  218.6 35.6 %all-to-all-start.3 = ((bf16[32,1,64,96]{3,2,1,0:T(8,128)(2,1)}), bf16[32,1,64,96]{3,2,1,0:T(8,128)(2,1)}, u32[]{:S(2)}, u32[]{:S(2)}) async-start(bf16[32,1,64,96]{3,2,1,0:T(8,128)(2,1)} %bitcast.14), calls=%async_computation.3 | async-start | bytes 1048576 | tf_op jit(solution)/shard_map/all_to_all | solution.py:119
  228.3 4.4 copy-start.3
  228.7 25.5 %copy-start.15 = (bf16[16,2,1,64,96]{4,1,0,3,2:T(2,128)(2,1)}, bf16[16,2,1,64,96]{4,1,0,3,2:T(2,128)(2,1)S(1)}, u32[]{:S(2)}) copy-start(bf16[16,2,1,64,96]{4,1,0,3,2:T(2,128)(2,1)S(1)} %copy.115) | copy-start | bytes 1179652
  230.2 38.0 %copy-start.25 = (f32[64,32]{1,0:T(8,128)}, f32[64,32]{1,0:T(8,128)S(1)}, u32[]{:S(2)}) copy-start(f32[64,32]{1,0:T(8,128)S(1)} %get-tuple-element.154) | copy-start | bytes 24580
  254.3 81.3 %all-to-all-start.13 = ((bf16[32,1,64,96]{3,2,1,0:T(8,128)(2,1)}), bf16[32,1,64,96]{3,2,1,0:T(8,128)(2,1)}, u32[]{:S(2)}, u32[]{:S(2)}) async-start(bf16[32,1,64,96]{3,2,1,0:T(8,128)(2,1)} %copy.126), calls=%async_computation.13 | async-start | bytes 1048576 | tf_op jit(solution)/shard_map/all_to_all | solution.py:150
  335.5 28.4 %all-to-all-start.4 = ((bf16[32,2,3072]{2,1,0:T(2,128)(2,1)}), bf16[32,2,3072]{2,1,0:T(2,128)(2,1)S(1)}, u32[]{:S(2)}, u32[]{:S(2)}) async-start(bf16[32,2,3072]{2,1,0:T(2,128)(2,1)} %reshape.213), calls=%async_computation.4 | async-start | bytes 786432 | tf_op jit(solution)/shard_map/all_to_all | solution.py:123
  364.0 27.5 %all-to-all-start.5 = ((bf16[32,2,3072]{2,1,0:T(2,128)(2,1)}), bf16[32,2,3072]{2,1,0:T(2,128)(2,1)S(1)}, u32[]{:S(2)}, u32[]{:S(2)}) async-start(bf16[32,2,3072]{2,1,0:T(2,128)(2,1)} %reshape.215), calls=%async_computation.5 | async-start | bytes 786432 | tf_op jit(solution)/shard_map/all_to_all | solution.py:124
  375.5 75.6 %copy-start.4 = (bf16[16,2,1,64,96]{4,1,0,3,2:T(2,128)(2,1)S(1)}, bf16[16,2,1,64,96]{4,1,0,3,2:T(2,128)(2,1)}, u32[]{:S(2)}) copy-start(bf16[16,2,1,64,96]{4,1,0,3,2:T(2,128)(2,1)} %copy-done.3) | copy-start | bytes 1179652
  391.4 19.5 %copy-start.9 = (bf16[32,2,3072]{2,1,0:T(2,128)(2,1)}, bf16[32,2,3072]{2,1,0:T(2,128)(2,1)S(1)}, u32[]{:S(2)}) copy-start(bf16[32,2,3072]{2,1,0:T(2,128)(2,1)S(1)} %all-to-all-done.5) | copy-start | bytes 1179652
  391.4 44.2 %all-to-all-start.9 = ((bf16[2,16,64,96]{3,0,2,1:T(2,128)(2,1)}), bf16[2,16,64,96]{3,0,2,1:T(2,128)(2,1)S(1)}, u32[]{:S(2)}, u32[]{:S(2)}) async-start(bf16[2,16,64,96]{3,0,2,1:T(2,128)(2,1)} %copy.117), calls=%async_computation.9 | async-start | bytes 1048576 | tf_op jit(solution)/shard_map/all_to_all | solution.py:142
  410.9 40.6 %copy-start.26 = (f32[64,32]{1,0:T(8,128)S(1)}, f32[64,32]{1,0:T(8,128)}, u32[]{:S(2)}) copy-start(f32[64,32]{1,0:T(8,128)} %copy-done.25) | copy-start | bytes 24580
  435.6 35.2 %all-to-all-start.6 = ((bf16[32,2,3072]{2,1,0:T(2,128)(2,1)}), bf16[32,2,3072]{2,1,0:T(2,128)(2,1)S(1)}, u32[]{:S(2)}, u32[]{:S(2)}) async-start(bf16[32,2,3072]{2,1,0:T(2,128)(2,1)} %reshape.217), calls=%async_computation.6 | async-start | bytes 786432 | tf_op jit(solution)/shard_map/all_to_all | solution.py:125
  451.5 28.5 %copy-start.16 = (bf16[16,2,1,64,96]{4,1,0,3,2:T(2,128)(2,1)S(1)}, bf16[16,2,1,64,96]{4,1,0,3,2:T(2,128)(2,1)}, u32[]{:S(2)}) copy-start(bf16[16,2,1,64,96]{4,1,0,3,2:T(2,128)(2,1)} %copy-done.15) | copy-start | bytes 1179652
  471.6 33.5 %all-to-all-start.11 = ((bf16[32,1,64,96]{3,2,1,0:T(8,128)(2,1)}), bf16[32,1,64,96]{3,2,1,0:T(8,128)(2,1)S(1)}, u32[]{:S(2)}, u32[]{:S(2)}) async-start(bf16[32,1,64,96]{3,2,1,0:T(8,128)(2,1)} %copy.122), calls=%async_computation.11 | async-start | bytes 1048576 | tf_op jit(solution)/shard_map/all_to_all | solution.py:146
  480.1 30.5 %copy-start.23 = (f32[1536]{0:T(1024)S(1)}, f32[1536]{0:T(1024)}, u32[]{:S(2)}) copy-start(f32[1536]{0:T(1024)} %get-tuple-element.151) | copy-start | bytes 18436
  482.1 31.6 %copy-start.10 = (bf16[32,2,3072]{2,1,0:T(2,128)(2,1)S(1)}, bf16[32,2,3072]{2,1,0:T(2,128)(2,1)}, u32[]{:S(2)}) copy-start(bf16[32,2,3072]{2,1,0:T(2,128)(2,1)} %copy-done.9) | copy-start | bytes 1179652
  505.9 23.5 %all-to-all-start.12 = ((bf16[32,1,64,96]{3,2,1,0:T(8,128)(2,1)}), bf16[32,1,64,96]{3,2,1,0:T(8,128)(2,1)S(1)}, u32[]{:S(2)}, u32[]{:S(2)}) async-start(bf16[32,1,64,96]{3,2,1,0:T(8,128)(2,1)} %copy.124), calls=%async_computation.12 | async-start | bytes 1048576 | tf_op jit(solution)/shard_map/all_to_all | solution.py:149
  518.7 11.4 %copy-start.8 = (bf16[2,64,1536]{2,1,0:T(8,128)(2,1)S(1)}, bf16[2,64,1536]{2,1,0:T(8,128)(2,1)}, u32[]{:S(2)}) copy-start(bf16[2,64,1536]{2,1,0:T(8,128)(2,1)} %param.17) | copy-start | bytes 1179652
  518.7 11.4 %copy-start.22 = (f32[1536]{0:T(1024)S(1)}, f32[1536]{0:T(1024)}, u32[]{:S(2)}) copy-start(f32[1536]{0:T(1024)} %param.22) | copy-start | bytes 18436
  521.7 9.3 %copy-start.24 = (f32[1,1536]{1,0:T(1,128)S(1)}, f32[1,1536]{1,0:T(1,128)}, u32[]{:S(2)}) copy-start(f32[1,1536]{1,0:T(1,128)} %stack.18) | copy-start | bytes 18436
  (21 other events, 49.2 us)
where the time goes:
time: 658 us; the launch traced here: 649 us
  waiting for transfers between devices  225 us (34%)
  starting transfers between devices  161 us (24%)
  blocking collectives  117 us (18%)
  other arithmetic  55.8 us (8%)
  matrix products  47 us (7%)
  local copies, waits for them, and re-layouts  41.6 us (6%)
    psum x1, blocking collectives, shards(): lax.psum((time_key_term, time_value_term), ('frame', 'space'))  117 us
    unnamed x5, other arithmetic  34.8 us
    all_to_all x1, starting transfers between devices, shards(): lax.all_to_all(query_items, 'space', split_axis=0, concat_axis=2, tiled=T...  28.2 us
    all_to_all x1, waiting for transfers between devices, shards(): lax.all_to_all(key_items, 'space', split_axis=0, concat_axis=2, tiled=True)  25.3 us
    all_to_all x1, waiting for transfers between devices, shards(): lax.all_to_all(query_items, 'space', split_axis=0, concat_axis=2, tiled=T...  25.3 us
    all_to_all x1, waiting for transfers between devices, shards(): lax.all_to_all(grad_items, 'space', split_axis=0, concat_axis=2, tiled=True)  24.2 us
    all_to_all x1, waiting for transfers between devices, shards(): lax.all_to_all(query_gradient, 'frame', split_axis=0, concat_axis=1, tile...  22 us
    all_to_all x1, waiting for transfers between devices, shards(): lax.all_to_all(value_items, 'space', split_axis=0, concat_axis=2, tiled=T...  21.5 us
  transfers between devices with their start and end apart: 14, of which 13 were waited for; matrix products, arithmetic and copies ran while one was open for 21% of the time, Pallas kernels for 0%

commit v1 on v0

v1 whole, which is shorter than its diff:
```python
import functools

import jax
import jax.numpy as jnp
from jax import lax
from jax.experimental import pallas as pl
from jax.experimental.pallas import tpu as pltpu
from jax.sharding import PartitionSpec as P

F32, BF16 = jnp.float32, jnp.bfloat16
H = 16
HD = 96
NS = 32
NF = 16
FL = 2
PL = 64
SEQ = NS * PL
ROWS = PL * HD // 128
SPAN = 512
QB = 256
KT = 256
SCALE = HD**-0.5
LOG2E = 1.4426950408889634
NT = (((1,), (1,)), ((), ()))
NN = (((1,), (0,)), ((), ()))
MESH = pl.DeviceIdType.MESH


def mm(a, b, dims):
    return lax.dot_general(a, b, dims, preferred_element_type=F32)


def lanes(shape):
    return lax.broadcasted_iota(jnp.int32, shape, len(shape) - 1)


def split_heads(x):
    a, b, c = x[:, 0:128], x[:, 128:256], x[:, 256:384]
    lane = lanes(a.shape)
    return (
        a,
        jnp.where(lane < 32, pltpu.roll(a, 32, 1), pltpu.roll(b, 32, 1)),
        jnp.where(lane < 64, pltpu.roll(b, 64, 1), pltpu.roll(c, 64, 1)),
        pltpu.roll(c, 96, 1),
    )


def join_heads(w, x, y, z):
    lane = lanes(w.shape)
    x, y, z = pltpu.roll(x, 96, 1), pltpu.roll(y, 64, 1), pltpu.roll(z, 32, 1)
    return jnp.where(lane < 96, w, x), jnp.where(lane < 64, x, y), jnp.where(lane < 32, y, z)


def pack_tiles(t0, t1, t2, t3):
    lane = lanes(t0.shape)
    return (
        jnp.where(lane < 96, t0, pltpu.roll(t3, 96, 1)),
        jnp.where(lane < 96, t1, pltpu.roll(t3, 64, 1)),
        jnp.where(lane < 96, t2, pltpu.roll(t3, 32, 1)),
    )


def unpack_tiles(p0, p1, p2):
    lane = lanes(p0.shape)
    zero = jnp.zeros_like(p0)
    last = jnp.where(lane < 32, pltpu.roll(p0, 32, 1), pltpu.roll(p1, 64, 1))
    last = jnp.where(lane < 64, last, pltpu.roll(p2, 96, 1))
    return tuple(jnp.where(lane < 96, t, zero) for t in (p0, p1, p2, last))


def tiles_of(ref, lead, count=3):
    return [ref[(*lead, pl.ds(16 * t, 16), slice(None))] for t in range(count)]


def attend(q, ks, vs, g, kt, dq, dk, dv, s_scr, p_scr, span, masked):
    tiles = span // KT
    for c in range(SEQ // 128):
        kt[:, c * 128 : (c + 1) * 128] = ks[c * 128 : (c + 1) * 128, :].T
    dk[...] = jnp.zeros_like(dk)
    dv[...] = jnp.zeros_like(dv)

    def step(start, base):
        rows = pl.ds(pl.multiple_of(start, QB), QB)
        keys = [pl.ds(pl.multiple_of(base + t * KT, KT), KT) for t in range(tiles)]
        tile = [pl.ds(t * KT, KT) for t in range(tiles)]
        qi, gi = q[rows, :], g[rows, :]
        if masked:
            key_pos = lax.broadcasted_iota(jnp.int32, (KT, QB), 0) & 15
            same = key_pos == (lanes((KT, QB)) & 15)
        top = None
        for t in range(tiles):
            s = mm(ks[keys[t], :], qi, NT)
            if masked:
                s = jnp.where(same, s, -jnp.inf)
            s_scr[tile[t], :] = s
            here = jnp.max(s.reshape(KT // 8, 8, QB), axis=0)
            top = here if top is None else jnp.maximum(top, here)
        top = jnp.max(top, axis=0, keepdims=True)
        total = jnp.zeros((8, QB), F32)
        delta = jnp.zeros((8, QB), F32)
        for t in range(tiles):
            e = jnp.exp2((s_scr[tile[t], :] - top) * (SCALE * LOG2E))
            dp = mm(vs[keys[t], :], gi, NT)
            s_scr[tile[t], :] = e
            p_scr[tile[t], :] = dp
            total += jnp.sum(e.reshape(KT // 8, 8, QB), axis=0)
            delta += jnp.sum((e * dp).reshape(KT // 8, 8, QB), axis=0)
        inv = 1.0 / jnp.sum(total, axis=0, keepdims=True)
        delta = jnp.sum(delta, axis=0, keepdims=True) * inv
        dq_t = jnp.zeros((HD, QB), F32)
        for t in range(tiles):
            p = s_scr[tile[t], :] * inv
            ds = (p * (p_scr[tile[t], :] - delta) * SCALE).astype(BF16)
            dv[keys[t], :] += mm(p.astype(BF16), gi, NN)
            dk[keys[t], :] += mm(ds, qi, NN)
            dq_t += mm(kt[0:HD, keys[t]], ds, NN)
        dq[rows, 0:HD] = dq_t.T.astype(BF16)

    def outer(b, carry):
        for i in range(span // QB if masked else 1):
            step(b * (span if masked else QB) + i * QB, b * span if masked else 0)
        return carry

    lax.fori_loop(0, SEQ // (span if masked else QB), outer, 0)


def kernel(
    q_s, k_s, v_s, q_t, k_t, v_t, grad, gain_ks, gain_vs, gain_kt, gain_vt,
    dq_s, dk_s, dv_s, dq_t, dk_t, dv_t, ia3,
    s_out, s_in, t_out, t_in, sb_out, sb_in, tb_out, tb_in,
    q, k, v, ks, vs, g, kt, dq, dk, dv, s_scr, p_scr, gains,
    a_out, as1, at1, as2, at2,
    send_sem, s_sem, t_sem, sb_sem, tb_sem, a_send, as1_sem, at1_sem, as2_sem, at2_sem,
):
    f = lax.axis_index("frame")
    s = lax.axis_index("space")
    z, y = s // 4, s % 4
    fx, fz, fc = f // 4, (f // 2) % 2, f % 2

    def space_id(i):
        zi, yi = i // 4, i % 4
        half = (z // 4 + 1 + zi // 4) % 2
        return (4 * half + (z + zi) % 4) * 4 + (y + yi) % 4

    def space_z(i):
        half = (z // 4 + 1 + i // 4) % 2
        return 4 * half + (z + i) % 4

    def frame_id(i):
        zi = (fz + 1 + i // 8) % 2
        return 4 * ((fx + i // 2) % 4) + 2 * zi + (fc + i) % 2

    def send(axis, me, to, src, dst, ssem, rsem):
        @pl.when(to != me)
        def _():
            pltpu.make_async_remote_copy(
                src.at[to], dst.at[me], ssem, rsem.at[me], device_id={axis: to}, device_id_type=MESH
            ).start()

        @pl.when(to == me)
        def _():
            pltpu.make_async_copy(src.at[me], dst.at[me], rsem.at[me]).start()

    def arrived(dst, rsem, j):
        pltpu.make_async_copy(dst.at[j], dst.at[j], rsem.at[j]).wait()

    def sent(src, n, sem):
        part = src.at[pl.ds(0, n - 1)]
        pltpu.make_async_copy(part, part, sem).wait()

    def loop(n, body):
        def run(i, carry):
            body(i)
            return carry

        lax.fori_loop(0, n, run, 0)

    barrier = pltpu.get_barrier_semaphore()

    def greet(axis, me, n):
        def body(i):
            pl.semaphore_signal(
                barrier, inc=1, device_id={axis: (me + 1 + i) % n}, device_id_type=MESH
            )

        loop(n - 1, body)

    greet("space", s, NS)
    greet("frame", f, NF)

    def gain_body(i):
        cols = pl.ds(pl.multiple_of(i * 384, 128), 384)
        for r, ref in enumerate((gain_ks, gain_vs, gain_kt, gain_vt)):
            heads = split_heads(jnp.broadcast_to(ref[:, cols], (8, 384)))
            for j in range(4):
                gains[r, 4 * i + j] = heads[j]

    loop(H // 4, gain_body)

    def pack_group(ref, fl, hg):
        cols = pl.ds(pl.multiple_of(hg * 384, 128), 384)
        heads = split_heads(ref[fl, :, cols])
        return [pack_tiles(*(x[16 * t : 16 * t + 16] for t in range(4))) for x in heads]

    def put(ref, lead, tiles):
        for t in range(3):
            ref[(*lead, pl.ds(16 * t, 16), slice(None))] = tiles[t]

    pl.semaphore_wait(barrier, NS + NF - 2)

    def space_pack(i):
        zi = space_z(i)
        fl, hg = zi // 4, zi % 4
        for n, ref in enumerate((q_s, k_s, v_s, grad)):
            packed = pack_group(ref, fl, hg)
            for j in range(4):
                put(s_out, (4 * zi + j, n), packed[j])
                if n == 3:
                    put(t_out, (4 * hg + j, fl, n), packed[j])
        for j in range(4):
            send("space", s, 4 * zi + (y + j) % 4, s_out, s_in, send_sem.at[0], s_sem)

    loop(8, space_pack)

    def time_pack(i):
        fl, hg = i // 4, i % 4
        for n, ref in enumerate((q_t, k_t, v_t)):
            packed = pack_group(ref, fl, hg)
            for j in range(4):
                put(t_out, (4 * hg + j, fl, n), packed[j])

    loop(8, time_pack)
    loop(NF, lambda i: send("frame", f, frame_id(i), t_out, t_in, send_sem.at[1], t_sem))

    def unpack_item(ref, lead, row_of, gain_k, gain_v):
        for n, dst in enumerate((q, k, v, g)):
            tiles = unpack_tiles(*tiles_of(ref, (*lead, n)))
            for t in range(4):
                rows = pl.ds(pl.multiple_of(row_of(t), 16), 16)
                dst[rows, :] = tiles[t]
                if n == 1:
                    ks[rows, :] = (tiles[t].astype(F32) * gain_k).astype(BF16)
                if n == 2:
                    vs[rows, :] = (tiles[t].astype(F32) * gain_v).astype(BF16)

    def pack_item(ref, lead, row_of, gain_k, gain_v):
        for n, src in enumerate((dq, dk, dv)):
            tiles = []
            for t in range(4):
                x = src[pl.ds(pl.multiple_of(row_of(t), 16), 16), :]
                if n:
                    gain = gain_k if n == 1 else gain_v
                    x = (x.astype(BF16).astype(F32) * gain).astype(BF16)
                tiles.append(x)
            put(ref, (*lead, n), pack_tiles(*tiles))

    def gain_rows(row, head):
        return gains[row, head, 0:1, :], gains[row + 1, head, 0:1, :]

    def terms(slot):
        def body(i, carry):
            rows = pl.ds(pl.multiple_of(i * 128, 128), 128)
            out = []
            for acc, a, b in ((carry[0], dk, k), (carry[1], dv, v)):
                prod = a[rows, :].astype(BF16).astype(F32) * b[rows, :].astype(F32)
                out.append(acc + jnp.sum(prod.reshape(16, 8, 128), axis=0))
            return tuple(out)

        zero = jnp.zeros((8, 128), F32)
        tk, tv = lax.fori_loop(0, SEQ // 128, body, (zero, zero))
        a_out[slot] = jnp.concatenate(
            [jnp.sum(tk, axis=0, keepdims=True), jnp.sum(tv, axis=0, keepdims=True), zero[2:]]
        )

    def share(axis, me, n, slot, dst, rsem):
        dst[me] = a_out[slot]

        def body(i):
            pltpu.make_async_remote_copy(
                a_out.at[slot],
                dst.at[me],
                a_send.at[slot],
                rsem.at[me],
                device_id={axis: (me + 1 + i) % n},
                device_id_type=MESH,
            ).start()

        loop(n - 1, body)

    def collect(me, n, dst, rsem):
        loop(n - 1, lambda i: arrived(dst, rsem, (me + 1 + i) % n))

    head = s % H
    gk, gv = gain_rows(0, head)

    def space_unpack(i):
        j = space_id(i)
        arrived(s_in, s_sem, j)
        unpack_item(s_in, (j,), lambda t: PL * j + 16 * t, gk, gv)

    loop(NS, space_unpack)
    dq[...] = jnp.zeros_like(dq)
    attend(q, ks, vs, g, kt, dq, dk, dv, s_scr, p_scr, SEQ, False)

    def space_back(i):
        j = space_id(i)
        pack_item(sb_out, (j,), lambda t: PL * j + 16 * t, gk, gv)
        send("space", s, j, sb_out, sb_in, send_sem.at[2], sb_sem)

    loop(NS, space_back)
    terms(0)
    share("frame", f, NF, 0, as1, as1_sem)

    gk2, gv2 = gain_rows(2, f)

    def time_unpack(i):
        j = frame_id(i)
        arrived(t_in, t_sem, j)
        for fl in range(FL):
            row = lambda t: SPAN * t + 16 * (FL * j + fl)
            unpack_item(t_in, (j, fl), row, gk2, gv2)

    loop(NF, time_unpack)
    attend(q, ks, vs, g, kt, dq, dk, dv, s_scr, p_scr, SPAN, True)
    terms(1)
    share("space", s, NS, 1, at1, at1_sem)

    def time_back(i):
        j = frame_id(i)
        for fl in range(FL):
            row = lambda t: SPAN * t + 16 * (FL * j + fl)
            pack_item(tb_out, (j, fl), row, gk2, gv2)
        send("frame", f, j, tb_out, tb_in, send_sem.at[3], tb_sem)

    loop(NF, time_back)

    collect(f, NF, as1, as1_sem)
    a_out[2] = jnp.sum(as1[...], axis=0)
    share("space", s, NS, 2, as2, as2_sem)
    collect(s, NS, at1, at1_sem)
    a_out[3] = jnp.sum(at1[...], axis=0)
    share("frame", f, NF, 3, at2, at2_sem)

    def unpack_group(ref, leads, dst, fl, hg):
        heads = [unpack_tiles(*tiles_of(ref, lead)) for lead in leads]
        for t in range(4):
            pieces = join_heads(*(h[t] for h in heads))
            for c in range(3):
                cols = pl.ds(pl.multiple_of(hg * 384 + c * 128, 128), 128)
                dst[fl, pl.ds(16 * t, 16), cols] = pieces[c]

    def space_home(i):
        zi = space_z(i)
        for j in range(4):
            arrived(sb_in, sb_sem, 4 * zi + j)
        for n, dst in enumerate((dq_s, dk_s, dv_s)):
            unpack_group(sb_in, [(4 * zi + j, n) for j in range(4)], dst, zi // 4, zi % 4)

    loop(8, space_home)

    norm = float(SEQ * NF * FL) ** -0.5
    collect(s, NS, as2, as2_sem)
    collect(f, NF, at2, at2_sem)
    for hg in range(H // 4):
        for c, piece in enumerate(join_heads(*(as2[4 * hg + j] + as2[H + 4 * hg + j] for j in range(4)))):
            col = hg * 384 + c * 128
            ia3[0:2, col : col + 128] = piece[0:2] * norm
        for c, piece in enumerate(join_heads(*(at2[4 * hg + j] for j in range(4)))):
            col = hg * 384 + c * 128
            ia3[2:4, col : col + 128] = piece[0:2] * norm

    def time_home(hg):
        for j in range(4):
            arrived(tb_in, tb_sem, 4 * hg + j)
        for fl in range(FL):
            for n, dst in enumerate((dq_t, dk_t, dv_t)):
                unpack_group(tb_in, [(4 * hg + j, fl, n) for j in range(4)], dst, fl, hg)

    loop(H // 4, time_home)

    sent(s_out, NS, send_sem.at[0])
    sent(t_out, NF, send_sem.at[1])
    sent(sb_out, NS, send_sem.at[2])
    sent(tb_out, NF, send_sem.at[3])
    sent(as1, NF, a_send.at[0])
    sent(at1, NS, a_send.at[1])
    sent(as2, NS, a_send.at[2])
    sent(at2, NF, a_send.at[3])


def shards(*args):
    full = jax.ShapeDtypeStruct((FL, PL, H * HD), BF16)
    vmem = pl.BlockSpec(memory_space=pltpu.VMEM)
    operands = list(args[:7]) + [a.reshape(1, H * HD) for a in args[7:]]

    def nat(dtype):
        return pltpu.VMEM((SEQ, 128), dtype)

    dma = pltpu.SemaphoreType.DMA
    scratch = [
        pltpu.VMEM((NS, 4, ROWS, 128), BF16),
        pltpu.VMEM((NS, 4, ROWS, 128), BF16),
        pltpu.VMEM((NF, FL, 4, ROWS, 128), BF16),
        pltpu.VMEM((NF, FL, 4, ROWS, 128), BF16),
        pltpu.VMEM((NS, 3, ROWS, 128), BF16),
        pltpu.VMEM((NS, 3, ROWS, 128), BF16),
        pltpu.VMEM((NF, FL, 3, ROWS, 128), BF16),
        pltpu.VMEM((NF, FL, 3, ROWS, 128), BF16),
        *[nat(BF16) for _ in range(6)],
        pltpu.VMEM((128, SEQ), BF16),
        nat(BF16),
        nat(F32),
        nat(F32),
        pltpu.VMEM((SEQ, QB), F32),
        pltpu.VMEM((SEQ, QB), F32),
        pltpu.VMEM((4, H, 8, 128), F32),
        pltpu.VMEM((4, 8, 128), F32),
        pltpu.VMEM((NF, 8, 128), F32),
        pltpu.VMEM((NS, 8, 128), F32),
        pltpu.VMEM((NS, 8, 128), F32),
        pltpu.VMEM((NF, 8, 128), F32),
        dma((4,)),
        dma((NS,)),
        dma((NF,)),
        dma((NS,)),
        dma((NF,)),
        dma((4,)),
        dma((NF,)),
        dma((NS,)),
        dma((NS,)),
        dma((NF,)),
    ]
    return pl.pallas_call(
        kernel,
        out_shape=[full] * 6 + [jax.ShapeDtypeStruct((4, H * HD), F32)],
        in_specs=[vmem] * 11,
        out_specs=[vmem] * 7,
        scratch_shapes=scratch,
        compiler_params=pltpu.CompilerParams(
            collective_id=0, has_side_effects=True, vmem_limit_bytes=48 * 1024 * 1024
        ),
    )(*operands)


def solution(mesh):
    split = P("frame", "space", None)
    return jax.shard_map(
        shards,
        mesh=mesh,
        in_specs=(split,) * 7 + (P(),) * 4,
        out_specs=(split,) * 6 + (P(),),
        check_vma=False,
    )
```

time: 658 us -> 298 us (0.45)
  the two profiles are of different devices: /device:TPU:1 before, /device:TPU:481 now
where the time goes in v1:
time: 298 us
  Pallas kernels  283 us (95%)
  local copies, waits for them, and re-layouts  14.1 us (5%)
    pallas_call x1, Pallas kernels, shards(): pl.pallas_call(kernel, out_shape=[full] * 6 + [jax.ShapeDtypeStruct((4, H...  283 us
    unnamed x27, local copies, waits for them, and re-layouts  13.4 us

profile of v1, /device:TPU:481, one launch (start us, length us, event | category | flops | bytes accessed | tf_op | source)
XLA Modules:
  0.0 297.9 jit_solution(10955349074828157734)
XLA Ops:
  0.6 0.0 copy-start.7
  0.6 0.7 reshape.26.gain_ks
  1.4 0.0 copy-done.7
  1.4 0.0 copy-start.8
  1.4 0.7 copy-done.8
  2.1 0.0 copy-start.9
  2.1 0.7 copy-done.9
  2.8 0.0 copy-start
  2.8 1.0 copy-done
  3.8 0.0 copy-start.1
  3.8 1.0 copy-done.1
  4.7 0.0 copy-start.2
  4.7 1.0 copy-done.2
  5.7 0.0 copy-start.3
  5.7 1.0 copy-done.3
  6.7 0.0 copy-start.4
  6.7 1.0 copy-done.4
  7.7 0.0 copy-start.5
  7.7 1.0 copy-done.5
  8.7 0.0 copy-start.6
  8.7 1.0 copy-done.6
  9.7 283.1 %shard_map.162 = (bf16[2,64,1536]{2,1,0:T(8,128)(2,1)S(1)}, bf16[2,64,1536]{2,1,0:T(8,128)(2,1)S(1)}, bf16[2,64,1536]{2,1,0:T(8,128)(2,1)S(1)}, bf16[2,64,1536]{...) custom-call(bf16[2,64,1536]{2,1,0:T(8,128)(2,1)S(1)} %copy-done, ...), custom_call_target="tpu_custom_call" | custom-call | tf_op jit(solution)/shard_map/pallas_call | solution.py:433
  292.8 0.7 copy.25
  293.6 0.7 copy.26
  294.3 0.7 copy.27
  295.1 0.7 copy.28
  295.8 0.7 copy.29
  296.5 0.7 copy.30
  297.3 0.6 copy.31
  (3 shorter events, 0.0 us)
Async XLA Ops:
  0.6 0.7 copy-start.7
  1.4 0.7 copy-start.8
  2.1 0.7 copy-start.9
  2.8 1.0 copy-start
  3.8 1.0 copy-start.1
  4.7 1.0 copy-start.2
  5.7 1.0 copy-start.3
  6.7 1.0 copy-start.4
  7.7 1.0 copy-start.5
  8.7 1.0 copy-start.6

commit v2 on v1

--- a/solution.py
+++ b/solution.py
@@ -19,6 +19,7 @@
 SPAN = 512
 QB = 256
 KT = 256
+VMEM_LIMIT = 123 * 2**19
 SCALE = HD**-0.5
 LOG2E = 1.4426950408889634
 NT = (((1,), (1,)), ((), ()))
@@ -125,8 +126,11 @@
 
 
 def kernel(
-    q_s, k_s, v_s, q_t, k_t, v_t, grad, gain_ks, gain_vs, gain_kt, gain_vt,
-    dq_s, dk_s, dv_s, dq_t, dk_t, dv_t, ia3,
+    q_s_hbm, k_s_hbm, v_s_hbm, q_t_hbm, k_t_hbm, v_t_hbm, grad_hbm,
+    gain_ks_hbm, gain_vs_hbm, gain_kt_hbm, gain_vt_hbm,
+    dq_s_hbm, dk_s_hbm, dv_s_hbm, dq_t_hbm, dk_t_hbm, dv_t_hbm, ia3_hbm,
+    q_s, k_s, v_s, q_t, k_t, v_t, grad, gain_ks, gain_vs, gain_kt, gain_vt, load_sem,
+    dq_s, dk_s, dv_s, dq_t, dk_t, dv_t, ia3, store_sem,
     s_out, s_in, t_out, t_in, sb_out, sb_in, tb_out, tb_in,
     q, k, v, ks, vs, g, kt, dq, dk, dv, s_scr, p_scr, gains,
     a_out, as1, at1, as2, at2,
@@ -175,6 +179,19 @@
 
         lax.fori_loop(0, n, run, 0)
 
+    names = ("grad", "q_s", "k_s", "v_s", "q_t", "k_t", "v_t")
+    loads = {}
+    for n, (name, src, dst) in enumerate(
+        zip(
+            names + ("gain_ks", "gain_vs", "gain_kt", "gain_vt"),
+            (grad_hbm, q_s_hbm, k_s_hbm, v_s_hbm, q_t_hbm, k_t_hbm, v_t_hbm)
+            + (gain_ks_hbm, gain_vs_hbm, gain_kt_hbm, gain_vt_hbm),
+            (grad, q_s, k_s, v_s, q_t, k_t, v_t, gain_ks, gain_vs, gain_kt, gain_vt),
+        )
+    ):
+        loads[name] = pltpu.make_async_copy(src, dst, load_sem.at[n])
+        loads[name].start()
+
     barrier = pltpu.get_barrier_semaphore()
 
     def greet(axis, me, n):
@@ -188,15 +205,6 @@
     greet("space", s, NS)
     greet("frame", f, NF)
 
-    def gain_body(i):
-        cols = pl.ds(pl.multiple_of(i * 384, 128), 384)
-        for r, ref in enumerate((gain_ks, gain_vs, gain_kt, gain_vt)):
-            heads = split_heads(jnp.broadcast_to(ref[:, cols], (8, 384)))
-            for j in range(4):
-                gains[r, 4 * i + j] = heads[j]
-
-    loop(H // 4, gain_body)
-
     def pack_group(ref, fl, hg):
         cols = pl.ds(pl.multiple_of(hg * 384, 128), 384)
         heads = split_heads(ref[fl, :, cols])
@@ -206,6 +214,8 @@
         for t in range(3):
             ref[(*lead, pl.ds(16 * t, 16), slice(None))] = tiles[t]
 
+    for name in names[:4]:
+        loads[name].wait()
     pl.semaphore_wait(barrier, NS + NF - 2)
 
     def space_pack(i):
@@ -215,22 +225,39 @@
             packed = pack_group(ref, fl, hg)
             for j in range(4):
                 put(s_out, (4 * zi + j, n), packed[j])
-                if n == 3:
-                    put(t_out, (4 * hg + j, fl, n), packed[j])
         for j in range(4):
             send("space", s, 4 * zi + (y + j) % 4, s_out, s_in, send_sem.at[0], s_sem)
 
     loop(8, space_pack)
 
+    for name in names[4:]:
+        loads[name].wait()
+
+    def frame_send(to):
+        send("frame", f, to, t_out, t_in, send_sem.at[1], t_sem)
+
     def time_pack(i):
-        fl, hg = i // 4, i % 4
-        for n, ref in enumerate((q_t, k_t, v_t)):
-            packed = pack_group(ref, fl, hg)
+        hg = (fx + i) % 4
+        for fl in range(FL):
+            for n, ref in enumerate((q_t, k_t, v_t, grad)):
+                packed = pack_group(ref, fl, hg)
+                for j in range(4):
+                    put(t_out, (4 * hg + j, fl, n), packed[j])
+        for j in range(2):
+            frame_send(4 * hg + 2 * (1 - fz) + (fc + j) % 2)
+
+    loop(4, time_pack)
+    loop(8, lambda i: frame_send(frame_id(8 + i)))
+
+    for name in ("gain_ks", "gain_vs", "gain_kt", "gain_vt"):
+        loads[name].wait()
+
+    for i in range(H // 4):
+        for r, ref in enumerate((gain_ks, gain_vs, gain_kt, gain_vt)):
+            heads = split_heads(jnp.broadcast_to(ref[384 * i : 384 * i + 384].reshape(1, 384), (8, 384)))
             for j in range(4):
-                put(t_out, (4 * hg + j, fl, n), packed[j])
-
-    loop(8, time_pack)
-    loop(NF, lambda i: send("frame", f, frame_id(i), t_out, t_in, send_sem.at[1], t_sem))
+                gains[r, 4 * i + j] = heads[j]
+
 
     def unpack_item(ref, lead, row_of, gain_k, gain_v):
         for n, dst in enumerate((q, k, v, g)):
@@ -269,7 +296,7 @@
         zero = jnp.zeros((8, 128), F32)
         tk, tv = lax.fori_loop(0, SEQ // 128, body, (zero, zero))
         a_out[slot] = jnp.concatenate(
-            [jnp.sum(tk, axis=0, keepdims=True), jnp.sum(tv, axis=0, keepdims=True), zero[2:]]
+            [jnp.sum(tk, axis=0, keepdims=True), jnp.sum(tv, axis=0, keepdims=True)]
         )
 
     def share(axis, me, n, slot, dst, rsem):
@@ -290,37 +317,42 @@
     def collect(me, n, dst, rsem):
         loop(n - 1, lambda i: arrived(dst, rsem, (me + 1 + i) % n))
 
-    head = s % H
-    gk, gv = gain_rows(0, head)
+    dq[...] = jnp.zeros_like(dq)
+
+    gk_s, gv_s = gain_rows(0, s % H)
 
     def space_unpack(i):
         j = space_id(i)
         arrived(s_in, s_sem, j)
-        unpack_item(s_in, (j,), lambda t: PL * j + 16 * t, gk, gv)
+        unpack_item(s_in, (j,), lambda t: PL * j + 16 * t, gk_s, gv_s)
 
     loop(NS, space_unpack)
-    dq[...] = jnp.zeros_like(dq)
     attend(q, ks, vs, g, kt, dq, dk, dv, s_scr, p_scr, SEQ, False)
+    terms(0)
+    share("frame", f, NF, 0, as1, as1_sem)
 
     def space_back(i):
         j = space_id(i)
-        pack_item(sb_out, (j,), lambda t: PL * j + 16 * t, gk, gv)
+        pack_item(sb_out, (j,), lambda t: PL * j + 16 * t, gk_s, gv_s)
         send("space", s, j, sb_out, sb_in, send_sem.at[2], sb_sem)
 
     loop(NS, space_back)
-    terms(0)
-    share("frame", f, NF, 0, as1, as1_sem)
-
-    gk2, gv2 = gain_rows(2, f)
+
+    gk_t, gv_t = gain_rows(2, f)
+
+    def time_row(j, fl):
+        return lambda t: SPAN * t + 16 * (FL * j + fl)
 
     def time_unpack(i):
         j = frame_id(i)
         arrived(t_in, t_sem, j)
         for fl in range(FL):
-            row = lambda t: SPAN * t + 16 * (FL * j + fl)
-            unpack_item(t_in, (j, fl), row, gk2, gv2)
+            unpack_item(t_in, (j, fl), time_row(j, fl), gk_t, gv_t)
 
     loop(NF, time_unpack)
+    collect(f, NF, as1, as1_sem)
+    a_out[2] = jnp.sum(as1[...], axis=0)
+    share("space", s, NS, 2, as2, as2_sem)
     attend(q, ks, vs, g, kt, dq, dk, dv, s_scr, p_scr, SPAN, True)
     terms(1)
     share("space", s, NS, 1, at1, at1_sem)
@@ -328,18 +360,10 @@
     def time_back(i):
         j = frame_id(i)
         for fl in range(FL):
-            row = lambda t: SPAN * t + 16 * (FL * j + fl)
-            pack_item(tb_out, (j, fl), row, gk2, gv2)
+            pack_item(tb_out, (j, fl), time_row(j, fl), gk_t, gv_t)
         send("frame", f, j, tb_out, tb_in, send_sem.at[3], tb_sem)
 
-    loop(NF, time_back)
-
-    collect(f, NF, as1, as1_sem)
-    a_out[2] = jnp.sum(as1[...], axis=0)
-    share("space", s, NS, 2, as2, as2_sem)
-    collect(s, NS, at1, at1_sem)
-    a_out[3] = jnp.sum(at1[...], axis=0)
-    share("frame", f, NF, 3, at2, at2_sem)
+    loop(NF // 4, time_back)
 
     def unpack_group(ref, leads, dst, fl, hg):
         heads = [unpack_tiles(*tiles_of(ref, lead)) for lead in leads]
@@ -349,6 +373,13 @@
                 cols = pl.ds(pl.multiple_of(hg * 384 + c * 128, 128), 128)
                 dst[fl, pl.ds(16 * t, 16), cols] = pieces[c]
 
+    stores = []
+
+    def store(src, dst):
+        copy = pltpu.make_async_copy(src, dst, store_sem.at[len(stores)])
+        copy.start()
+        stores.append(copy)
+
     def space_home(i):
         zi = space_z(i)
         for j in range(4):
@@ -357,17 +388,13 @@
             unpack_group(sb_in, [(4 * zi + j, n) for j in range(4)], dst, zi // 4, zi % 4)
 
     loop(8, space_home)
-
-    norm = float(SEQ * NF * FL) ** -0.5
+    for src, dst in ((dq_s, dq_s_hbm), (dk_s, dk_s_hbm), (dv_s, dv_s_hbm)):
+        store(src, dst)
+    collect(s, NS, at1, at1_sem)
+    a_out[3] = jnp.sum(at1[...], axis=0)
+    share("frame", f, NF, 3, at2, at2_sem)
+    loop(NF - NF // 4, lambda i: time_back(NF // 4 + i))
     collect(s, NS, as2, as2_sem)
-    collect(f, NF, at2, at2_sem)
-    for hg in range(H // 4):
-        for c, piece in enumerate(join_heads(*(as2[4 * hg + j] + as2[H + 4 * hg + j] for j in range(4)))):
-            col = hg * 384 + c * 128
-            ia3[0:2, col : col + 128] = piece[0:2] * norm
-        for c, piece in enumerate(join_heads(*(at2[4 * hg + j] for j in range(4)))):
-            col = hg * 384 + c * 128
-            ia3[2:4, col : col + 128] = piece[0:2] * norm
 
     def time_home(hg):
         for j in range(4):
@@ -377,6 +404,19 @@
                 unpack_group(tb_in, [(4 * hg + j, fl, n) for j in range(4)], dst, fl, hg)
 
     loop(H // 4, time_home)
+    for src, dst in ((dq_t, dq_t_hbm), (dk_t, dk_t_hbm), (dv_t, dv_t_hbm)):
+        store(src, dst)
+
+    norm = float(SEQ * NF * FL) ** -0.5
+    collect(f, NF, at2, at2_sem)
+    for hg in range(H // 4):
+        space = [as2[4 * hg + j] + as2[H + 4 * hg + j] for j in range(4)]
+        time = [at2[4 * hg + j] for j in range(4)]
+        for row, heads in ((0, space), (2, time)):
+            for c, piece in enumerate(join_heads(*heads)):
+                col = hg * 384 + c * 128
+                ia3[row : row + 2, col : col + 128] = piece * norm
+    store(ia3, ia3_hbm)
 
     sent(s_out, NS, send_sem.at[0])
     sent(t_out, NF, send_sem.at[1])
@@ -386,18 +426,39 @@
     sent(at1, NS, a_send.at[1])
     sent(as2, NS, a_send.at[2])
     sent(at2, NF, a_send.at[3])
+    for copy in stores:
+        copy.wait()
+
+
+def write_out(*refs):
+    n = len(refs) // 3
+    sems = refs[-1]
+    loads = [pltpu.make_async_copy(refs[i], refs[2 * n + i], sems.at[i]) for i in range(n)]
+    stores = [pltpu.make_async_copy(refs[2 * n + i], refs[n + i], sems.at[n + i]) for i in range(n)]
+    for load in loads:
+        load.start()
+    for load, store in zip(loads, stores):
+        load.wait()
+        store.start()
+    for store in stores:
+        store.wait()
 
 
 def shards(*args):
     full = jax.ShapeDtypeStruct((FL, PL, H * HD), BF16)
-    vmem = pl.BlockSpec(memory_space=pltpu.VMEM)
-    operands = list(args[:7]) + [a.reshape(1, H * HD) for a in args[7:]]
+    hbm = pl.BlockSpec(memory_space=pltpu.HBM)
 
     def nat(dtype):
         return pltpu.VMEM((SEQ, 128), dtype)
 
     dma = pltpu.SemaphoreType.DMA
     scratch = [
+        *[pltpu.VMEM((FL, PL, H * HD), BF16) for _ in range(7)],
+        *[pltpu.VMEM((H * HD,), F32) for _ in range(4)],
+        dma((11,)),
+        *[pltpu.VMEM((FL, PL, H * HD), BF16) for _ in range(6)],
+        pltpu.VMEM((4, H * HD), F32),
+        dma((7,)),
         pltpu.VMEM((NS, 4, ROWS, 128), BF16),
         pltpu.VMEM((NS, 4, ROWS, 128), BF16),
         pltpu.VMEM((NF, FL, 4, ROWS, 128), BF16),
@@ -414,11 +475,7 @@
         pltpu.VMEM((SEQ, QB), F32),
         pltpu.VMEM((SEQ, QB), F32),
         pltpu.VMEM((4, H, 8, 128), F32),
-        pltpu.VMEM((4, 8, 128), F32),
-        pltpu.VMEM((NF, 8, 128), F32),
-        pltpu.VMEM((NS, 8, 128), F32),
-        pltpu.VMEM((NS, 8, 128), F32),
-        pltpu.VMEM((NF, 8, 128), F32),
+        *[pltpu.VMEM((n, 2, 128), F32) for n in (4, NF, NS, NS, NF)],
         dma((4,)),
         dma((NS,)),
         dma((NF,)),
@@ -430,16 +487,25 @@
         dma((NS,)),
         dma((NF,)),
     ]
-    return pl.pallas_call(
+    out_shape = [full] * 6 + [jax.ShapeDtypeStruct((4, H * HD), F32)]
+    results = pl.pallas_call(
         kernel,
-        out_shape=[full] * 6 + [jax.ShapeDtypeStruct((4, H * HD), F32)],
-        in_specs=[vmem] * 11,
-        out_specs=[vmem] * 7,
+        out_shape=out_shape,
+        in_specs=[hbm] * 11,
+        out_specs=[hbm] * 7,
         scratch_shapes=scratch,
         compiler_params=pltpu.CompilerParams(
-            collective_id=0, has_side_effects=True, vmem_limit_bytes=48 * 1024 * 1024
+            collective_id=0, has_side_effects=True, vmem_limit_bytes=VMEM_LIMIT
         ),
-    )(*operands)
+    )(*args)
+    return pl.pallas_call(
+        write_out,
+        out_shape=out_shape,
+        in_specs=[hbm] * 7,
+        out_specs=[hbm] * 7,
+        scratch_shapes=[pltpu.VMEM(a.shape, a.dtype) for a in out_shape] + [dma((14,))],
+        compiler_params=pltpu.CompilerParams(vmem_limit_bytes=VMEM_LIMIT),
+    )(*results)
 
 
 def solution(mesh):

time: 298 us -> 273 us (0.916)
  local copies, waits for them, and re-layouts: 14.1 us -> 0 us
  Pallas kernels: 283 us -> 271 us
    unnamed x27 -> x0, local copies, waits for them, and re-layouts: 13.4 us -> none
    pallas_call x1 -> x2, Pallas kernels: 283 us -> 271 us  [the longest x1 269 us: shards(): pl.pallas_call(kernel, out_shape=out_shape, in_specs=[hbm] * 11, out_spec...]
where the time goes in v2:
time: 273 us; the launch traced here: 272 us
  Pallas kernels  271 us (99%)
    pallas_call x1, Pallas kernels, shards(): pl.pallas_call(kernel, out_shape=out_shape, in_specs=[hbm] * 11, out_spec...  269 us

profile of v2, /device:TPU:481, one launch (start us, length us, event | category | flops | bytes accessed | tf_op | source)
XLA Modules:
  0.0 271.9 jit_solution(15445506147855542309)
XLA Ops:
  0.6 268.7 %shard_map.162 = (bf16[2,64,1536]{2,1,0:T(8,128)(2,1)}, bf16[2,64,1536]{2,1,0:T(8,128)(2,1)}, bf16[2,64,1536]{2,1,0:T(8,128)(2,1)}, bf16[2,64,1536]{2,1,0:T(8,12...) custom-call(bf16[2,64,1536]{2,1,0:T(8,128)(2,1)} %q_s_hbm.1, ...), custom_call_target="tpu_custom_call" | custom-call | tf_op jit(solution)/shard_map/pallas_call | solution.py:491
  269.3 2.5 shard_map.163

commit v3 on v2

--- a/solution.py
+++ b/solution.py
@@ -1,3 +1,5 @@
+import functools
+
 import functools
 
 import jax
@@ -131,24 +133,33 @@
     dq_s_hbm, dk_s_hbm, dv_s_hbm, dq_t_hbm, dk_t_hbm, dv_t_hbm, ia3_hbm,
     q_s, k_s, v_s, q_t, k_t, v_t, grad, gain_ks, gain_vs, gain_kt, gain_vt, load_sem,
     dq_s, dk_s, dv_s, dq_t, dk_t, dv_t, ia3, store_sem,
-    s_out, s_in, t_out, t_in, sb_out, sb_in, tb_out, tb_in,
+    s_out, s_in, t_out, t_in, tg_out, tg_in, sb_out, sb_in, tb_out, tb_in,
     q, k, v, ks, vs, g, kt, dq, dk, dv, s_scr, p_scr, gains,
-    a_out, as1, at1, as2, at2,
-    send_sem, s_sem, t_sem, sb_sem, tb_sem, a_send, as1_sem, at1_sem, as2_sem, at2_sem,
+    a_out, a_out2, as1, at1, as2, at2,
+    tg_sem, send_sem, s_sem, t_sem, sb_sem, tb_sem, a_send, as1_sem, at1_sem, as2_sem, at2_sem,
 ):
     f = lax.axis_index("frame")
     s = lax.axis_index("space")
     z, y = s // 4, s % 4
     fx, fz, fc = f // 4, (f // 2) % 2, f % 2
+    half = s // 16
+    s_set, s_fl, s_place = (half + fz) % 2, (s // 8) % 2, s % 8
+    t_set, t_place = (fz + half) % 2, 2 * fx + fc
+
+    def group_of_z(zi):
+        return (zi // 2) % 2, 2 * ((zi // 4 + fz) % 2) + zi % 2
+
+    def frame_of(hg, j):
+        return 4 * (2 * (hg % 2) + j // 2) + 2 * ((hg // 2 + half) % 2) + j % 2
 
     def space_id(i):
         zi, yi = i // 4, i % 4
-        half = (z // 4 + 1 + zi // 4) % 2
-        return (4 * half + (z + zi) % 4) * 4 + (y + yi) % 4
+        zi_half = (z // 4 + 1 + zi // 4) % 2
+        return (4 * zi_half + (z + zi) % 4) * 4 + (y + yi) % 4
 
     def space_z(i):
-        half = (z // 4 + 1 + i // 4) % 2
-        return 4 * half + (z + i) % 4
+        zi_half = (z // 4 + 1 + i // 4) % 2
+        return 4 * zi_half + (z + i) % 4
 
     def frame_id(i):
         zi = (fz + 1 + i // 8) % 2
@@ -205,6 +216,13 @@
     greet("space", s, NS)
     greet("frame", f, NF)
 
+    def greet_items(i):
+        at = {"frame": 4 * (i // 4) + 2 * (1 - fz) + (i // 2) % 2}
+        at["space"] = 16 * (1 - half) + 8 * (i % 2) + t_place
+        pl.semaphore_signal(barrier, inc=1, device_id=at, device_id_type=MESH)
+
+    loop(16, greet_items)
+
     def pack_group(ref, fl, hg):
         cols = pl.ds(pl.multiple_of(hg * 384, 128), 384)
         heads = split_heads(ref[fl, :, cols])
@@ -216,11 +234,11 @@
 
     for name in names[:4]:
         loads[name].wait()
-    pl.semaphore_wait(barrier, NS + NF - 2)
+    pl.semaphore_wait(barrier, NS + NF - 2 + 16)
 
     def space_pack(i):
         zi = space_z(i)
-        fl, hg = zi // 4, zi % 4
+        fl, hg = group_of_z(zi)
         for n, ref in enumerate((q_s, k_s, v_s, grad)):
             packed = pack_group(ref, fl, hg)
             for j in range(4):
@@ -233,21 +251,27 @@
     for name in names[4:]:
         loads[name].wait()
 
-    def frame_send(to):
-        send("frame", f, to, t_out, t_in, send_sem.at[1], t_sem)
-
-    def time_pack(i):
-        hg = (fx + i) % 4
+    def time_pack(hg):
         for fl in range(FL):
             for n, ref in enumerate((q_t, k_t, v_t, grad)):
                 packed = pack_group(ref, fl, hg)
                 for j in range(4):
-                    put(t_out, (4 * hg + j, fl, n), packed[j])
-        for j in range(2):
-            frame_send(4 * hg + 2 * (1 - fz) + (fc + j) % 2)
+                    if n == 3:
+                        put(tg_out, (frame_of(hg, j), fl), packed[j])
+                    else:
+                        put(t_out, (frame_of(hg, j), fl, n), packed[j])
 
     loop(4, time_pack)
-    loop(8, lambda i: frame_send(frame_id(8 + i)))
+
+    def time_send(i):
+        send("frame", f, frame_id(i), t_out, t_in, send_sem.at[1], t_sem)
+
+    def time_send_near(i):
+        time_send(8 + i)
+        send("frame", f, frame_id(8 + i), tg_out, tg_in, send_sem.at[4], tg_sem)
+
+    loop(8, time_send)
+    loop(8, time_send_near)
 
     for name in ("gain_ks", "gain_vs", "gain_kt", "gain_vt"):
         loads[name].wait()
@@ -259,9 +283,9 @@
                 gains[r, 4 * i + j] = heads[j]
 
 
-    def unpack_item(ref, lead, row_of, gain_k, gain_v):
+    def unpack_item(leads, row_of, gain_k, gain_v):
         for n, dst in enumerate((q, k, v, g)):
-            tiles = unpack_tiles(*tiles_of(ref, (*lead, n)))
+            tiles = unpack_tiles(*tiles_of(*leads[n]))
             for t in range(4):
                 rows = pl.ds(pl.multiple_of(row_of(t), 16), 16)
                 dst[rows, :] = tiles[t]
@@ -299,12 +323,12 @@
             [jnp.sum(tk, axis=0, keepdims=True), jnp.sum(tv, axis=0, keepdims=True)]
         )
 
-    def share(axis, me, n, slot, dst, rsem):
-        dst[me] = a_out[slot]
+    def share(axis, me, n, block, slot, dst, rsem):
+        dst[me] = block[...]
 
         def body(i):
             pltpu.make_async_remote_copy(
-                a_out.at[slot],
+                block,
                 dst.at[me],
                 a_send.at[slot],
                 rsem.at[me],
@@ -319,17 +343,31 @@
 
     dq[...] = jnp.zeros_like(dq)
 
-    gk_s, gv_s = gain_rows(0, s % H)
+    gk_s, gv_s = gain_rows(0, 8 * s_set + s_place)
 
     def space_unpack(i):
         j = space_id(i)
         arrived(s_in, s_sem, j)
-        unpack_item(s_in, (j,), lambda t: PL * j + 16 * t, gk_s, gv_s)
-
-    loop(NS, space_unpack)
+        unpack_item([(s_in, (j, n)) for n in range(4)], lambda t: PL * j + 16 * t, gk_s, gv_s)
+
+    def space_unpack_far(i):
+        space_unpack(i)
+        j = space_id(i)
+        at = {"frame": 4 * (s_place // 2) + 2 * (1 - fz) + s_place % 2, "space": j}
+        pltpu.make_async_remote_copy(
+            s_in.at[j, 3],
+            tg_in.at[f, s_fl],
+            send_sem.at[5],
+            tg_sem.at[f],
+            device_id=at,
+            device_id_type=MESH,
+        ).start()
+
+    loop(NS // 2, space_unpack_far)
+    loop(NS // 2, lambda i: space_unpack(NS // 2 + i))
     attend(q, ks, vs, g, kt, dq, dk, dv, s_scr, p_scr, SEQ, False)
     terms(0)
-    share("frame", f, NF, 0, as1, as1_sem)
+    share("frame", f, NF, a_out.at[0], 0, as1, as1_sem)
 
     def space_back(i):
         j = space_id(i)
@@ -338,7 +376,7 @@
 
     loop(NS, space_back)
 
-    gk_t, gv_t = gain_rows(2, f)
+    gk_t, gv_t = gain_rows(2, 8 * t_set + t_place)
 
     def time_row(j, fl):
         return lambda t: SPAN * t + 16 * (FL * j + fl)
@@ -346,16 +384,20 @@
     def time_unpack(i):
         j = frame_id(i)
         arrived(t_in, t_sem, j)
+        arrived(tg_in, tg_sem, j)
         for fl in range(FL):
-            unpack_item(t_in, (j, fl), time_row(j, fl), gk_t, gv_t)
+            leads = [(t_in, (j, fl, n)) for n in range(3)] + [(tg_in, (j, fl))]
+            unpack_item(leads, time_row(j, fl), gk_t, gv_t)
 
     loop(NF, time_unpack)
     collect(f, NF, as1, as1_sem)
-    a_out[2] = jnp.sum(as1[...], axis=0)
-    share("space", s, NS, 2, as2, as2_sem)
+    for r in range(2):
+        parts = [as1[4 * x + 2 * r + c] for x in range(4) for c in range(2)]
+        a_out2[0, 2 * r : 2 * r + 2, :] = functools.reduce(jnp.add, parts)
+    share("space", s, NS, a_out2.at[0], 2, as2, as2_sem)
     attend(q, ks, vs, g, kt, dq, dk, dv, s_scr, p_scr, SPAN, True)
     terms(1)
-    share("space", s, NS, 1, at1, at1_sem)
+    share("space", s, NS, a_out.at[1], 1, at1, at1_sem)
 
     def time_back(i):
         j = frame_id(i)
@@ -384,24 +426,26 @@
         zi = space_z(i)
         for j in range(4):
             arrived(sb_in, sb_sem, 4 * zi + j)
+        fl, hg = group_of_z(zi)
         for n, dst in enumerate((dq_s, dk_s, dv_s)):
-            unpack_group(sb_in, [(4 * zi + j, n) for j in range(4)], dst, zi // 4, zi % 4)
+            unpack_group(sb_in, [(4 * zi + j, n) for j in range(4)], dst, fl, hg)
 
     loop(8, space_home)
     for src, dst in ((dq_s, dq_s_hbm), (dk_s, dk_s_hbm), (dv_s, dv_s_hbm)):
         store(src, dst)
     collect(s, NS, at1, at1_sem)
-    a_out[3] = jnp.sum(at1[...], axis=0)
-    share("frame", f, NF, 3, at2, at2_sem)
+    for b in range(2):
+        a_out2[1, 2 * b : 2 * b + 2, :] = jnp.sum(at1[16 * b : 16 * b + 16], axis=0)
+    share("frame", f, NF, a_out2.at[1], 3, at2, at2_sem)
     loop(NF - NF // 4, lambda i: time_back(NF // 4 + i))
     collect(s, NS, as2, as2_sem)
 
     def time_home(hg):
         for j in range(4):
-            arrived(tb_in, tb_sem, 4 * hg + j)
+            arrived(tb_in, tb_sem, frame_of(hg, j))
         for fl in range(FL):
             for n, dst in enumerate((dq_t, dk_t, dv_t)):
-                unpack_group(tb_in, [(4 * hg + j, fl, n) for j in range(4)], dst, fl, hg)
+                unpack_group(tb_in, [(frame_of(hg, j), fl, n) for j in range(4)], dst, fl, hg)
 
     loop(H // 4, time_home)
     for src, dst in ((dq_t, dq_t_hbm), (dk_t, dk_t_hbm), (dv_t, dv_t_hbm)):
@@ -410,8 +454,16 @@
     norm = float(SEQ * NF * FL) ** -0.5
     collect(f, NF, at2, at2_sem)
     for hg in range(H // 4):
-        space = [as2[4 * hg + j] + as2[H + 4 * hg + j] for j in range(4)]
-        time = [at2[4 * hg + j] for j in range(4)]
+        e, space, time = hg // 2, [], []
+        for j in range(4):
+            place = 4 * (hg % 2) + j
+            here, there = 16 * e + place, 16 * (1 - e) + place
+            space.append(
+                (as2[here, 0:2, :] + as2[here + 8, 0:2, :])
+                + (as2[there, 2:4, :] + as2[there + 8, 2:4, :])
+            )
+            peer = 4 * (place // 2) + place % 2
+            time.append(at2[peer + 2 * e, 0:2, :] + at2[peer + 2 * (1 - e), 2:4, :])
         for row, heads in ((0, space), (2, time)):
             for c, piece in enumerate(join_heads(*heads)):
                 col = hg * 384 + c * 128
@@ -420,6 +472,8 @@
 
     sent(s_out, NS, send_sem.at[0])
     sent(t_out, NF, send_sem.at[1])
+    sent(tg_out, 8, send_sem.at[4])
+    sent(tg_in, 9, send_sem.at[5])
     sent(sb_out, NS, send_sem.at[2])
     sent(tb_out, NF, send_sem.at[3])
     sent(as1, NF, a_send.at[0])
@@ -461,8 +515,10 @@
         dma((7,)),
         pltpu.VMEM((NS, 4, ROWS, 128), BF16),
         pltpu.VMEM((NS, 4, ROWS, 128), BF16),
-        pltpu.VMEM((NF, FL, 4, ROWS, 128), BF16),
-        pltpu.VMEM((NF, FL, 4, ROWS, 128), BF16),
+        pltpu.VMEM((NF, FL, 3, ROWS, 128), BF16),
+        pltpu.VMEM((NF, FL, 3, ROWS, 128), BF16),
+        pltpu.VMEM((NF, FL, ROWS, 128), BF16),
+        pltpu.VMEM((NF, FL, ROWS, 128), BF16),
         pltpu.VMEM((NS, 3, ROWS, 128), BF16),
         pltpu.VMEM((NS, 3, ROWS, 128), BF16),
         pltpu.VMEM((NF, FL, 3, ROWS, 128), BF16),
@@ -475,8 +531,9 @@
         pltpu.VMEM((SEQ, QB), F32),
         pltpu.VMEM((SEQ, QB), F32),
         pltpu.VMEM((4, H, 8, 128), F32),
-        *[pltpu.VMEM((n, 2, 128), F32) for n in (4, NF, NS, NS, NF)],
-        dma((4,)),
+        *[pltpu.VMEM((n, r, 128), F32) for n, r in ((2, 2), (2, 4), (NF, 2), (NS, 2), (NS, 4), (NF, 4))],
+        dma((NF,)),
+        dma((6,)),
         dma((NS,)),
         dma((NF,)),
         dma((NS,)),

time: 273 us -> 263 us (0.963)
  Pallas kernels: 271 us -> 259 us
    pallas_call x1, Pallas kernels: 269 us -> 256 us  [shards(): pl.pallas_call(kernel, out_shape=out_shape, in_specs=[hbm] * 11, out_spec...]
where the time goes in v3:
time: 263 us; the launch traced here: 259 us
  Pallas kernels  259 us (98%)
    pallas_call x1, Pallas kernels, shards(): pl.pallas_call(kernel, out_shape=out_shape, in_specs=[hbm] * 11, out_spec...  256 us

profile of v3, /device:TPU:481, one launch (start us, length us, event | category | flops | bytes accessed | tf_op | source)
XLA Modules:
  0.0 259.5 jit_solution(7177150787338115961)
XLA Ops:
  0.6 256.3 %shard_map.162 = (bf16[2,64,1536]{2,1,0:T(8,128)(2,1)}, bf16[2,64,1536]{2,1,0:T(8,128)(2,1)}, bf16[2,64,1536]{2,1,0:T(8,128)(2,1)}, bf16[2,64,1536]{2,1,0:T(8,12...) custom-call(bf16[2,64,1536]{2,1,0:T(8,128)(2,1)} %q_s_hbm.1, ...), custom_call_target="tpu_custom_call" | custom-call | tf_op jit(solution)/shard_map/pallas_call | solution.py:548
  256.9 2.5 shard_map.163

commit v4 on v3

--- a/solution.py
+++ b/solution.py
@@ -22,6 +22,7 @@
 QB = 256
 KT = 256
 VMEM_LIMIT = 123 * 2**19
+EARLY = 5
 SCALE = HD**-0.5
 LOG2E = 1.4426950408889634
 NT = (((1,), (1,)), ((), ()))
@@ -405,7 +406,7 @@
             pack_item(tb_out, (j, fl), time_row(j, fl), gk_t, gv_t)
         send("frame", f, j, tb_out, tb_in, send_sem.at[3], tb_sem)
 
-    loop(NF // 4, time_back)
+    loop(EARLY, time_back)
 
     def unpack_group(ref, leads, dst, fl, hg):
         heads = [unpack_tiles(*tiles_of(ref, lead)) for lead in leads]
@@ -437,7 +438,7 @@
     for b in range(2):
         a_out2[1, 2 * b : 2 * b + 2, :] = jnp.sum(at1[16 * b : 16 * b + 16], axis=0)
     share("frame", f, NF, a_out2.at[1], 3, at2, at2_sem)
-    loop(NF - NF // 4, lambda i: time_back(NF // 4 + i))
+    loop(NF - EARLY, lambda i: time_back(EARLY + i))
     collect(s, NS, as2, as2_sem)
 
     def time_home(hg):

time: 263 us -> 262 us (level)
  no operation moved by 1% of the time
where the time goes in v4:
time: 262 us; the launch traced here: 258 us
  Pallas kernels  257 us (98%)
    pallas_call x1, Pallas kernels, shards(): pl.pallas_call(kernel, out_shape=out_shape, in_specs=[hbm] * 11, out_spec...  255 us

profile of v4, /device:TPU:481, one launch (start us, length us, event | category | flops | bytes accessed | tf_op | source)
XLA Modules:
  0.0 257.9 jit_solution(15488366329789406566)
XLA Ops:
  0.6 254.7 %shard_map.162 = (bf16[2,64,1536]{2,1,0:T(8,128)(2,1)}, bf16[2,64,1536]{2,1,0:T(8,128)(2,1)}, bf16[2,64,1536]{2,1,0:T(8,128)(2,1)}, bf16[2,64,1536]{2,1,0:T(8,12...) custom-call(bf16[2,64,1536]{2,1,0:T(8,128)(2,1)} %q_s_hbm.1, ...), custom_call_target="tpu_custom_call" | custom-call | tf_op jit(solution)/shard_map/pallas_call | solution.py:549
  255.4 2.5 shard_map.163
